TPU v7x, 32 devices: a whole 2x2x4 slice. The times are simulated.
32 devices in a mesh: groups: 2 (over x), dev: 16 (over z, y, core).
Axes of the slice: x: 2, y: 2, z: 4, core: 2. Of those that a mesh axis runs over, the one named last changes fastest.
Arguments:
- residual: bfloat16 [128, 3072], P('groups', 'dev'), parts along dimension 0, may hold values from -6 to 6
- queries: bfloat16 [32, 32, 768], P(('groups', 'dev')), parts along dimension 0, may hold values from -6 to 6
- kv_cache: bfloat16 [32, 2, 32, 128, 128], P(('groups', 'dev')), parts along dimension 0, may hold values from -6 to 6
- lengths: int32 [128], P('groups'), parts along dimension 0, may hold values from 2 to 128, as said below
- out_weight: bfloat16 [6144, 3072], P(None, 'dev'), may hold values from -0.078125 to 0.078125
- norm_gain: bfloat16 [3072], P('dev'), may hold values from 0.099609375 to 1.8984375
- router_weight: bfloat16 [3072, 8], P('dev'), may hold values from -0.109375 to 0.109375
- gate_weight: bfloat16 [3072, 65536], P(None, 'dev'), may hold values from -0.109375 to 0.109375
- up_weight: bfloat16 [3072, 65536], P(None, 'dev'), may hold values from -0.109375 to 0.109375
- down_weight: bfloat16 [65536, 3072], P('dev'), may hold values from -0.0625 to 0.0625
- expert_ids: int32 [128, 2], P('groups'), parts along dimension 0, may hold values from 0 to 7, all different within a row; in each aligned block of 64 rows (0 to 63, 64 to 127, ...) at most 32 rows name the same one
Outputs:
- layer_out: bfloat16 [128, 3072], P('groups', 'dev'), parts along dimension 0
There are 2 independent parts, one for each index of `groups`. A program takes and returns all parts, laid end to end along the dimension named above; an argument that names none is the same for every part. Nothing has to cross between parts.
Inputs may be any that keep to these rules, and one draw needn't show every extreme that they name: Positions from lengths[r] on are unused; some row has all 128 positions valid. `expert_ids`: each row names two different experts; no expert is named by more than 32 rows, a bound that some block reaches.
All inputs are finite; a program needn't handle non-finite values.
Results may differ from a plain program's by a relative error of at most 0.0048.
Values may be sent and summed in bfloat16 or wider, within the bound.
A program may use at most 192 MiB of HBM per device.

v0:
```python
import math

import jax
import jax.numpy as jnp
from jax import lax
from jax.sharding import PartitionSpec as P

D = 3072
KVHEADS = 8
HEAD_DIM = 128
EXPERTS = 8
GROUP_Q = 6


def attend(query_block, cache_block, row_lengths):
    shard_rows = query_block.shape[0]
    query_heads = query_block.reshape(shard_rows, GROUP_Q, HEAD_DIM)
    key_block = cache_block[0]
    value_block = cache_block[1]
    scores = jnp.einsum(
        "thd,tld->thl", query_heads, key_block, preferred_element_type=jnp.float32
    ) / math.sqrt(HEAD_DIM)
    positions = jnp.arange(key_block.shape[1])
    valid = positions[None, None, :] < row_lengths[:, None, None]
    scores = jnp.where(valid, scores, -1e30)
    row_top = jnp.max(scores, axis=2, keepdims=True)
    expo = jnp.where(valid, jnp.exp(scores - row_top), 0.0)
    probs = (expo / jnp.sum(expo, axis=2, keepdims=True)).astype(jnp.bfloat16)
    mixed_heads = jnp.einsum("thl,tld->thd", probs, value_block, preferred_element_type=jnp.float32)
    return mixed_heads.reshape(shard_rows, GROUP_Q * HEAD_DIM).astype(jnp.bfloat16)


def slot_tables(expert_ids, logits, slot_count):
    numbers = jnp.arange(EXPERTS)
    pick_first = (expert_ids[:, 0:1] == numbers[None, :]).astype(jnp.float32)
    pick_second = (expert_ids[:, 1:2] == numbers[None, :]).astype(jnp.float32)
    logit_first = jnp.sum(logits * pick_first, axis=1)
    logit_second = jnp.sum(logits * pick_second, axis=1)
    gate_first = 1.0 / (1.0 + jnp.exp(logit_second - logit_first))
    gate_second = 1.0 / (1.0 + jnp.exp(logit_first - logit_second))
    routed = pick_first + pick_second
    gate_table = pick_first * gate_first[:, None] + pick_second * gate_second[:, None]
    ranks = jnp.cumsum(routed, axis=0) - routed
    slot_numbers = jnp.arange(slot_count).astype(jnp.float32)
    slot_table = routed.T[:, None, :] * (ranks.T[:, None, :] == slot_numbers[None, :, None]).astype(
        jnp.float32
    )
    slot_gate = jnp.einsum("esb,be->es", slot_table, gate_table, precision=lax.Precision.HIGHEST)
    return (slot_table, slot_gate)


def integer_ranks(expert_ids):
    numbers = jnp.arange(EXPERTS, dtype=jnp.int32)
    routed_int = (expert_ids[:, 0:1] == numbers[None, :]).astype(jnp.int32) + (
        expert_ids[:, 1:2] == numbers[None, :]
    ).astype(jnp.int32)
    ranks_int = jnp.cumsum(routed_int, axis=0) - routed_int
    return (routed_int, ranks_int)


def run_expert(slot_in, gate_weight, up_weight, down_weight, weights_here):
    gate_part = jnp.dot(slot_in, gate_weight, preferred_element_type=jnp.float32)
    up_part = jnp.dot(slot_in, up_weight, preferred_element_type=jnp.float32)
    activation = (jax.nn.silu(gate_part) * up_part).astype(jnp.bfloat16)
    expert_out = jnp.dot(activation, down_weight, preferred_element_type=jnp.float32)
    return expert_out * weights_here[:, None]


def on_device(
    residual,
    queries,
    kv_cache,
    lengths,
    out_weight,
    norm_gain,
    router_weight,
    gate_weight,
    up_weight,
    down_weight,
    expert_ids,
):
    devices = lax.axis_size("dev")
    my_index = lax.axis_index("dev")
    shard_rows = queries.shape[1]
    group_width = queries.shape[2]
    batch_rows = residual.shape[0]
    column_count = residual.shape[1]
    slot_count = batch_rows // 2
    per_expert = devices // EXPERTS
    my_expert = my_index // per_expert
    row_lengths = lax.dynamic_slice_in_dim(lengths, my_index // KVHEADS * shard_rows, shard_rows)
    heads_local = attend(queries[0], kv_cache[0], row_lengths)
    gathered = lax.all_gather(heads_local, "dev", axis=0, tiled=True)
    gathered = gathered.reshape(devices // KVHEADS, KVHEADS, shard_rows, group_width)
    weight_blocks = out_weight.reshape(KVHEADS, group_width, column_count)
    attended = jnp.einsum(
        "bgtk,gkc->btc", gathered, weight_blocks, preferred_element_type=jnp.float32
    )
    attended = attended.reshape(batch_rows, column_count)
    hidden_state = residual.astype(jnp.float32) + attended
    gain_cols = norm_gain.astype(jnp.float32)[None, :]
    router_cols = router_weight.astype(jnp.float32)
    squares_local = jnp.sum(hidden_state * hidden_state, axis=1)
    square_total = lax.psum(squares_local, "dev")
    scale = lax.rsqrt(square_total / D + 1e-05)
    normed = hidden_state * scale[:, None] * gain_cols
    logits = lax.psum(jnp.dot(normed, router_cols, precision=lax.Precision.HIGHEST), "dev")
    expert_in = normed.astype(jnp.bfloat16)
    slot_table, slot_gate = slot_tables(expert_ids, logits, slot_count)
    routed_int, ranks_int = integer_ranks(expert_ids)
    weights_here = lax.dynamic_index_in_dim(slot_gate, my_expert, 0, keepdims=False)
    picked = jnp.einsum(
        "esb,bc->sec",
        slot_table.astype(jnp.bfloat16),
        expert_in,
        preferred_element_type=jnp.float32,
    ).astype(jnp.bfloat16)
    outgoing = jnp.broadcast_to(
        picked[:, :, None, :], (slot_count, EXPERTS, per_expert, column_count)
    )
    outgoing = outgoing.reshape(slot_count, devices * column_count)
    slot_in = lax.all_to_all(outgoing, "dev", split_axis=1, concat_axis=1, tiled=True)
    expert_out = run_expert(slot_in, gate_weight, up_weight, down_weight, weights_here)
    returned = lax.all_to_all(expert_out, "dev", split_axis=1, concat_axis=1, tiled=True)
    summed = jnp.sum(returned.reshape(slot_count, EXPERTS, per_expert, column_count), axis=2)
    first_expert = expert_ids[:, 0]
    second_expert = expert_ids[:, 1]
    first_rank = jnp.take_along_axis(ranks_int, first_expert[:, None], axis=1)[:, 0]
    second_rank = jnp.take_along_axis(ranks_int, second_expert[:, None], axis=1)[:, 0]
    moe = summed[first_rank, first_expert] + summed[second_rank, second_expert]
    return (hidden_state + moe).astype(jnp.bfloat16)


def solution(mesh):
    in_specs = (
        P("groups", "dev"),
        P(("groups", "dev"), None, None),
        P(("groups", "dev"), None, None, None, None),
        P("groups"),
        P(None, "dev"),
        P("dev"),
        P("dev", None),
        P(None, "dev"),
        P(None, "dev"),
        P("dev", None),
        P("groups", None),
    )
    out_specs = P("groups", "dev")
    return jax.shard_map(
        on_device, mesh=mesh, in_specs=in_specs, out_specs=out_specs, check_vma=False
    )
```

profile of v0, /device:TPU:0, one launch (start us, length us, event | category | flops | bytes accessed | tf_op | source)
XLA Modules:
  0.0 161.8 jit_solution(1836379037039901783)
XLA Ops:
  0.0 0.0 copy-start
  0.0 0.7 dynamic_slice.7
  0.7 0.1 iota_compare_fusion
  0.8 0.9 reshape_squeeze.3
  1.7 2.0 %fusion.62 = (f32[32,6]{1,0:T(8,128)S(1)}, f32[32,6,128]{2,1,0:T(8,128)S(1)}) fusion(pred[32,128]{1,0:T(8,128)(4,1)S(1)} %iota_compare_fusion, bf16[32,6,128]{2,1,0:T(8,128)(2,1)S(1)} %reshape_squeeze.3, bf16[1,2,32,128,128]{4,3,2,1,0:T(8,128)(2,1)} %param.15), kind=kOutput, calls=%fused_computation.102 | convolution fusion | flops 6414463 | bytes 1221376 | tf_op jit(solution)/shard_map/sub | solution.py:27
  3.7 1.7 %convolution_convert_fusion.1 = bf16[32,6,128]{2,1,0:T(8,128)(2,1)S(1)} fusion(bf16[1,2,32,128,128]{4,3,2,1,0:T(8,128)(2,1)} %param.15, f32[32,6,128]{2,1,0:T(8,128)S(1)} %get-tuple-element.23, f32[32,6]{1,0:T(8,128)S(1)} %get-tuple-element.22), kind=kOutput, calls=%fused_computation.18 | convolution fusion | flops 6365184 | bytes 1196800 | tf_op jit(solution)/shard_map/thl,tld->thd/dot_general | solution.py:29
  5.4 25.5 %all_gather.3 = bf16[512,768]{1,0:T(8,128)(2,1)S(1)} all-gather(bf16[32,768]{1,0:T(8,128)(2,1)S(1)} %bitcast.90), channel_id=1, replica_groups=mesh['groups'=2,'dev'=16] {'dev'}, dimensions={0}, use_global_device_ids=true | all-gather | bytes 835584 | tf_op jit(solution)/shard_map/all_gather | solution.py:93
  30.9 0.1 copy.56
  31.0 2.6 %multiply_reduce_fusion = (f32[64]{0:T(128)S(1)}, f32[64,192]{1,0:T(8,128)S(1)}) fusion(bf16[64,8,768]{2,0,1:T(8,128)(2,1)S(1)} %bitcast.89, bf16[24,8,8,768]{3,2,1,0:T(8,128)(2,1)} %bitcast.93, bf16[64,192]{1,0:T(8,128)(2,1)} %param.13), kind=kOutput, calls=%fused_computation.45 | convolution fusion | flops 151044032 | bytes 3219712 | tf_op jit(solution)/shard_map/bgtk,gkc->btc/dot_general | solution.py:96
  33.6 29.8 %psum.14 = f32[64]{0:T(128)S(1)} all-reduce(f32[64]{0:T(128)S(1)} %get-tuple-element.24), channel_id=1, replica_groups=mesh['groups'=2,'dev'=16] {'dev'}, use_global_device_ids=true, to_apply=%region_3.4 | all-reduce | flops 64 | bytes 512 | tf_op jit(solution)/shard_map/psum | solution.py:104
  63.5 0.7 convert_element_type.74
  64.1 0.0 copy-done
  64.1 0.2 fusion.38
  64.3 29.5 %psum.15 = f32[64,8]{0,1:T(8,128)S(1)} all-reduce(f32[64,8]{0,1:T(8,128)S(1)} %fusion.38), channel_id=1, replica_groups=mesh['groups'=2,'dev'=16] {'dev'}, use_global_device_ids=true, to_apply=%region_5.6 | all-reduce | flops 512 | bytes 4096 | tf_op jit(solution)/shard_map/psum | solution.py:107
  93.8 0.8 fusion.61
  94.6 0.1 copy.58
  94.7 0.1 reduce_window_sum.24
  94.8 0.1 copy.59
  94.9 0.2 fusion.9
  95.1 0.7 broadcast_in_dim.25
  95.8 3.5 %all-to-all-start = ((bf16[32,16,192]{2,0,1:T(8,128)(2,1)}), bf16[32,16,192]{2,0,1:T(8,128)(2,1)S(1)}, u32[]{:S(2)}, u32[]{:S(2)}) async-start(bf16[32,16,192]{2,0,1:T(8,128)(2,1)} %bitcast.11), calls=%async_computation | async-start | bytes 524288 | tf_op jit(solution)/shard_map/all_to_all | solution.py:122
  99.4 0.1 copy.62
  99.5 0.1 reduce_window_sum.26
  99.6 0.1 copy.63
  99.7 0.4 fusion.26
  100.1 9.3 %all-to-all-done = bf16[32,16,192]{2,0,1:T(8,128)(2,1)S(1)} async-done(((bf16[32,16,192]{2,0,1:T(8,128)(2,1)}), bf16[32,16,192]{2,0,1:T(8,128)(2,1)S(1)}, u32[]{:S(2)}, u32[]{:S(2)}) %all-to-all-start) | async-done | bytes 196640 | tf_op jit(solution)/shard_map/all_to_all | solution.py:122
  109.4 0.1 copy.60
  109.5 0.3 all_to_all.16
  109.8 10.4 %fusion.65 = f32[32,4096]{1,0:T(8,128)S(1)} fusion(bf16[32,3072]{1,0:T(8,128)(2,1)S(1)} %all_to_all.16, bf16[3072,4096]{1,0:T(8,128)(2,1)} %param.20), kind=kOutput, calls=%fused_computation.103 | convolution fusion | flops 805306368 | bytes 25886720 | tf_op jit(solution)/shard_map/dot_general | solution.py:62
  120.2 0.0 copy-start.1
  120.2 19.9 %convolution_multiply_fusion.1 = f32[32,3072]{1,0:T(8,128)S(1)} fusion(bf16[4096,3072]{1,0:T(8,128)(2,1)} %param.22, bf16[32,3072]{1,0:T(8,128)(2,1)S(1)} %all_to_all.16, bf16[3072,4096]{1,0:T(8,128)(2,1)} %param.21, f32[32,4096]{1,0:T(8,128)S(1)} %fusion.65, f32[32]{0:T(128)S(1)} %dynamic-slice_bitcast_fusion), kind=kOutput, calls=%fused_computation.7 | convolution fusion | flops 1611497472 | bytes 51445888 | tf_op jit(solution)/shard_map/dot_general | solution.py:65
  140.1 0.2 all_to_all.17
  140.4 1.1 copy.61
  141.5 3.6 %all-to-all-start.1 = ((f32[32,16,192]{2,0,1:T(8,128)}), f32[32,16,192]{2,0,1:T(8,128)S(1)}, u32[]{:S(2)}, u32[]{:S(2)}) async-start(f32[32,16,192]{2,0,1:T(8,128)} %copy.61), calls=%async_computation.1 | async-start | bytes 1048576 | tf_op jit(solution)/shard_map/all_to_all | solution.py:124
  145.1 0.7 gather_fusion.2
  145.8 0.7 gather_fusion.3
  146.6 0.0 copy-done.1
  146.6 12.9 %all-to-all-done.1 = f32[32,16,192]{2,0,1:T(8,128)S(1)} async-done(((f32[32,16,192]{2,0,1:T(8,128)}), f32[32,16,192]{2,0,1:T(8,128)S(1)}, u32[]{:S(2)}, u32[]{:S(2)}) %all-to-all-start.1) | async-done | bytes 393248 | tf_op jit(solution)/shard_map/all_to_all | solution.py:124
  159.5 0.2 copy.64
  159.7 0.8 gather_fusion.1
  160.4 0.8 gather_fusion
  161.2 0.6 add_convert_fusion
  (15 shorter events, 0.2 us)
Async XLA Ops:
  0.0 64.1 %copy-start = (bf16[192,8]{0,1:T(8,128)(2,1)S(1)}, bf16[192,8]{0,1:T(8,128)(2,1)}, u32[]{:S(2)}) copy-start(bf16[192,8]{0,1:T(8,128)(2,1)} %param.19) | copy-start | bytes 9220
  95.8 13.5 %all-to-all-start = ((bf16[32,16,192]{2,0,1:T(8,128)(2,1)}), bf16[32,16,192]{2,0,1:T(8,128)(2,1)S(1)}, u32[]{:S(2)}, u32[]{:S(2)}) async-start(bf16[32,16,192]{2,0,1:T(8,128)(2,1)} %bitcast.11), calls=%async_computation | async-start | bytes 524288 | tf_op jit(solution)/shard_map/all_to_all | solution.py:122
  120.2 26.3 %copy-start.1 = (s32[64,2]{0,1:T(2,128)S(1)}, s32[64,2]{0,1:T(2,128)}, u32[]{:S(2)}) copy-start(s32[64,2]{0,1:T(2,128)} %param.23) | copy-start | bytes 1540
  141.5 18.0 %all-to-all-start.1 = ((f32[32,16,192]{2,0,1:T(8,128)}), f32[32,16,192]{2,0,1:T(8,128)S(1)}, u32[]{:S(2)}, u32[]{:S(2)}) async-start(f32[32,16,192]{2,0,1:T(8,128)} %copy.61), calls=%async_computation.1 | async-start | bytes 1048576 | tf_op jit(solution)/shard_map/all_to_all | solution.py:124
where the time goes:
time: 162 us
  blocking collectives  84.8 us (52%)
  matrix products  37.5 us (23%)
  waiting for transfers between devices  22.2 us (14%)
  local copies, waits for them, and re-layouts  7.57 us (5%)
  starting transfers between devices  7.1 us (4%)
  other arithmetic  2.46 us (2%)
    psum x1, blocking collectives, on_device(): square_total = lax.psum(squares_local, 'dev')  29.8 us
    psum x1, blocking collectives, on_device(): lax.psum(jnp.dot(normed, router_cols, precision=lax.Precision.HIGHEST), '...  29.5 us
    all_gather x1, blocking collectives, on_device(): gathered = lax.all_gather(heads_local, 'dev', axis=0, tiled=True)  25.5 us
    dot_general x1, matrix products, run_expert(): jnp.dot(activation, down_weight, preferred_element_type=jnp.float32)  19.9 us
    all_to_all x1, waiting for transfers between devices, on_device(): lax.all_to_all(expert_out, 'dev', split_axis=1, concat_axis=1, tiled=True)  12.9 us
    dot_general x1, matrix products, run_expert(): jnp.dot(slot_in, gate_weight, preferred_element_type=jnp.float32)  10.4 us
    all_to_all x1, waiting for transfers between devices, on_device(): lax.all_to_all(outgoing, 'dev', split_axis=1, concat_axis=1, tiled=True)  9.32 us
    all_to_all x1, starting transfers between devices, on_device(): lax.all_to_all(expert_out, 'dev', split_axis=1, concat_axis=1, tiled=True)  3.57 us
  transfers between devices with their start and end apart: 2, of which 2 were waited for; matrix products, arithmetic and copies ran while one was open for 1% of the time, Pallas kernels for 0%

commit v1 on v0

--- a/solution.py
+++ b/solution.py
@@ -3,6 +3,8 @@
 import jax
 import jax.numpy as jnp
 from jax import lax
+from jax.experimental import pallas as pl
+from jax.experimental.pallas import tpu as pltpu
 from jax.sharding import PartitionSpec as P
 
 D = 3072
@@ -131,7 +133,484 @@
     return (hidden_state + moe).astype(jnp.bfloat16)
 
 
+ZS = 4
+YS = 2
+CHIPS = ZS * YS
+DEVS = 2 * CHIPS
+ROWS = 64
+SLOTS = 32
+BLOCK_ROWS = 32
+COLS = 192
+PAIR = 2 * COLS
+HALF_W = 256
+HEADS_W = GROUP_Q * HEAD_DIM
+FF_LOCAL = 4096
+FF_STEP = 512
+FF_STEPS = FF_LOCAL // FF_STEP
+UP_SLOTS = 6
+DOWN_SLOTS = 5
+F32 = jnp.float32
+BF16 = jnp.bfloat16
+NT = (((1,), (1,)), ((), ()))
+
+
+def iota(shape, dim):
+    return lax.broadcasted_iota(jnp.int32, shape, dim)
+
+
+def fused_kernel(
+    lengths,
+    ids,
+    residual,
+    gain,
+    router,
+    q_hbm,
+    kv_hbm,
+    ow_hbm,
+    gate_hbm,
+    up_hbm,
+    down_hbm,
+    out,
+    q_in,
+    kv,
+    ow,
+    gu,
+    dn,
+    qs,
+    lens,
+    heads,
+    gt,
+    wide,
+    picks,
+    xb,
+    stat_out,
+    stats,
+    xfull,
+    act,
+    rs,
+    ret,
+    in_sem,
+    gu_sem,
+    dn_sem,
+    h_send,
+    h_recv,
+    x_send,
+    x_recv,
+    s_send,
+    s_recv,
+    r_send,
+    r_recv,
+):
+    me = lax.axis_index("dev")
+    core = lax.rem(me, 2)
+    chip = me // 2
+    y = lax.rem(chip, YS)
+    z = chip // YS
+    sibling = chip * 2 + (1 - core)
+
+    def dev_of(zz, yy, cc):
+        return (zz * YS + yy) * 2 + cc
+
+    def remote(source, target, send, recv, device):
+        return pltpu.make_async_remote_copy(
+            src_ref=source,
+            dst_ref=target,
+            send_sem=send,
+            recv_sem=recv,
+            device_id={"dev": device},
+            device_id_type=pl.DeviceIdType.MESH,
+        )
+
+    q_copy = pltpu.make_async_copy(q_hbm.at[0], q_in, in_sem.at[0])
+    kv_copy = pltpu.make_async_copy(kv_hbm.at[0], kv, in_sem.at[1])
+    ow_copy = pltpu.make_async_copy(ow_hbm, ow, in_sem.at[2])
+    q_copy.start()
+    kv_copy.start()
+
+    barrier = pltpu.get_barrier_semaphore()
+    for k in range(1, DEVS):
+        pl.semaphore_signal(
+            barrier,
+            inc=1,
+            device_id={"dev": lax.rem(me + k, DEVS)},
+            device_id_type=pl.DeviceIdType.MESH,
+        )
+
+    def gu_copy(j, which):
+        slot = lax.rem(j, UP_SLOTS)
+        start = pl.multiple_of(j * FF_STEP, FF_STEP)
+        origin = up_hbm if which else gate_hbm
+        return pltpu.make_async_copy(
+            origin.at[:, pl.ds(start, FF_STEP)], gu.at[slot, which], gu_sem.at[slot, which]
+        )
+
+    def down_chip(d):
+        return lax.rem(chip + d + 1, CHIPS)
+
+    def dn_copy(d):
+        slot = lax.rem(d, DOWN_SLOTS)
+        start = pl.multiple_of(down_chip(d) * PAIR, 128)
+        return pltpu.make_async_copy(
+            down_hbm.at[:, pl.ds(start, PAIR)], dn.at[slot], dn_sem.at[slot]
+        )
+
+    my_rows = (me // KVHEADS) * BLOCK_ROWS
+    for t in range(BLOCK_ROWS):
+        lens[t] = jnp.full((8, 128), lengths[my_rows + t], jnp.int32)
+
+    lane = iota((ROWS, 128), 1)
+    routed = jnp.where((ids[:, 0:1] == lane) | (ids[:, 1:2] == lane), 1.0, 0.0)
+    tri = jnp.where(iota((ROWS, ROWS), 0) > iota((ROWS, ROWS), 1), 1.0, 0.0).astype(BF16)
+    rank = jnp.dot(tri, routed.astype(BF16), preferred_element_type=F32)
+    code = (routed * (rank + 1.0)).astype(BF16)
+    owner = iota((128, EXPERTS * SLOTS), 0) * SLOTS
+    place = iota((128, EXPERTS * SLOTS), 1)
+    spread = jnp.where((place >= owner) & (place < owner + SLOTS), 1.0, 0.0).astype(BF16)
+    spread_code = jnp.dot(code, spread, preferred_element_type=F32)
+    slot_number = (jnp.bitwise_and(iota((ROWS, EXPERTS * SLOTS), 1), SLOTS - 1) + 1).astype(F32)
+    table = jnp.where(spread_code == slot_number, 1.0, 0.0)
+    table_pad = jnp.concatenate([table, jnp.zeros_like(table)], axis=0)
+    gt[...] = jnp.transpose(table_pad)
+    routed_pad = jnp.concatenate([routed, jnp.zeros_like(routed)], axis=0).astype(BF16)
+
+    q_copy.wait()
+    qs[...] = jnp.zeros_like(qs)
+    for j in range(GROUP_Q):
+        qs[:, j, :] = q_in[:, j * HEAD_DIM : (j + 1) * HEAD_DIM].astype(F32)
+    kv_copy.wait()
+    ow_copy.start()
+    for j in range(UP_SLOTS):
+        gu_copy(j, 0).start()
+        gu_copy(j, 1).start()
+    for d in range(DOWN_SLOTS):
+        dn_copy(d).start()
+
+    scores = jnp.einsum(
+        "thd,tld->thl", qs[...].astype(BF16), kv[0], preferred_element_type=F32
+    ) * (1.0 / math.sqrt(HEAD_DIM))
+    valid = iota((BLOCK_ROWS, 8, 128), 2) < lens[...]
+    scores = jnp.where(valid, scores, -1e30)
+    top = jnp.max(scores, axis=2, keepdims=True)
+    expo = jnp.where(valid, jnp.exp(scores - top), 0.0)
+    probs = (expo / jnp.sum(expo, axis=2, keepdims=True)).astype(BF16)
+    qs[...] = jnp.einsum("thl,tld->thd", probs, kv[1], preferred_element_type=F32)
+    for j in range(GROUP_Q):
+        heads[me, :, j * HEAD_DIM : (j + 1) * HEAD_DIM] = qs[:, j, :].astype(BF16)
+
+    pl.semaphore_wait(barrier, DEVS - 1)
+
+    def head_copy(block, number, device):
+        return remote(
+            heads.at[block], heads.at[block], h_send.at[number], h_recv.at[block], device
+        )
+
+    sent = []
+
+    def send_heads(block, device):
+        copy = head_copy(block, len(sent), device)
+        copy.start()
+        sent.append(copy)
+
+    for k in (2, 1, 3):
+        send_heads(me, dev_of(lax.rem(z + k, ZS), y, core))
+    send_heads(me, dev_of(z, 1 - y, core))
+    send_heads(me, sibling)
+    for k in (1, 3, 2):
+        block = dev_of(lax.rem(z + k, ZS), y, core)
+        head_copy(block, 0, sibling).wait_recv()
+        send_heads(block, dev_of(z, 1 - y, core))
+        send_heads(block, sibling)
+    for k in (0, 1, 3, 2):
+        block = dev_of(lax.rem(z + k, ZS), 1 - y, core)
+        head_copy(block, 0, sibling).wait_recv()
+        send_heads(block, sibling)
+    for k in (0, 1, 3, 2):
+        for yy in (y, 1 - y):
+            block = dev_of(lax.rem(z + k, ZS), yy, 1 - core)
+            head_copy(block, 0, sibling).wait_recv()
+
+    ow_copy.wait()
+    attended = jnp.zeros((ROWS, COLS), F32)
+    for g in range(KVHEADS):
+        both = jnp.concatenate([heads[g], heads[KVHEADS + g]], axis=0)
+        attended += jnp.dot(
+            both, ow[g * HEADS_W : (g + 1) * HEADS_W, :], preferred_element_type=F32
+        )
+    hidden = residual[...].astype(F32) + attended
+    gained = hidden * gain[...].astype(F32)
+
+    wide[...] = jnp.zeros_like(wide)
+    wide[0:ROWS, 0:COLS] = gained
+    shifted = pltpu.roll(wide[...], core * 64, 1)
+    picked = jnp.dot(gt[...].astype(BF16), shifted.astype(BF16), preferred_element_type=F32)
+    picks[...] = picked.astype(BF16).reshape(EXPERTS, SLOTS, HALF_W)
+
+    router_cols = jnp.transpose(
+        jnp.concatenate([router[...].astype(F32), jnp.zeros((COLS, 120), F32)], axis=1)
+    )[0:8]
+    none = jnp.zeros_like(hidden)
+    stat_out[...] = lax.dot_general(
+        router_cols,
+        jnp.concatenate([gained, none], axis=0),
+        NT,
+        precision=lax.Precision.HIGHEST,
+        preferred_element_type=F32,
+    ) + lax.dot_general(
+        jnp.ones((8, COLS), F32),
+        jnp.concatenate([none, hidden * hidden], axis=0),
+        NT,
+        precision=lax.Precision.HIGHEST,
+        preferred_element_type=F32,
+    )
+
+    sent_x = []
+
+    def row_copies(cc, source_chip, source, stat_source, number, device):
+        at = cc * CHIPS + source_chip
+        return (
+            remote(source, xb.at[cc, source_chip], x_send.at[number], x_recv.at[at], device),
+            remote(stat_source, stats.at[cc, source_chip], s_send.at[number], s_recv.at[at], device),
+        )
+
+    def send_rows(cc, source_chip, source, stat_source, device):
+        copies = row_copies(cc, source_chip, source, stat_source, len(sent_x), device)
+        for copy in copies:
+            copy.start()
+        sent_x.append(copies)
+
+    def wait_rows(cc, source_chip):
+        for copy in row_copies(
+            cc, source_chip, xb.at[cc, source_chip], stats.at[cc, source_chip], 0, sibling
+        ):
+            copy.wait_recv()
+
+    for k in (4, 3, 5, 2, 6, 1, 7):
+        to = lax.rem(chip + k, CHIPS)
+        send_rows(core, chip, picks.at[to], stat_out, to * 2 + core)
+    send_rows(core, chip, picks.at[chip], stat_out, sibling)
+    xb[core, chip] = picks[chip]
+    stats[core, chip] = stat_out[...]
+    for k in (1, 7, 2, 6, 3, 5, 4):
+        source_chip = lax.rem(chip + k, CHIPS)
+        wait_rows(core, source_chip)
+        send_rows(
+            core,
+            source_chip,
+            xb.at[core, source_chip],
+            stats.at[core, source_chip],
+            sibling,
+        )
+    for k in (0, 1, 7, 2, 6, 3, 5, 4):
+        wait_rows(1 - core, lax.rem(chip + k, CHIPS))
+
+    for s in range(CHIPS):
+        at = s * PAIR
+        xfull[:, at : at + 128] = xb[0, s, :, 0:128]
+        xfull[:, at + 128 : at + 256] = xb[0, s, :, 128:256] + xb[1, s, :, 0:128]
+        xfull[:, at + 256 : at + 384] = xb[1, s, :, 128:256]
+    total = jnp.sum(stats[...].reshape(DEVS, 8, 128), axis=0)
+    total = jnp.concatenate([total, jnp.zeros((120, 128), F32)], axis=0)
+    mine = gt[pl.ds(pl.multiple_of(chip * SLOTS, SLOTS), SLOTS), :]
+    slot_logits = lax.dot_general(
+        mine, total, NT, precision=lax.Precision.HIGHEST, preferred_element_type=F32
+    )
+    slot_squares = lax.dot_general(
+        pltpu.roll(mine, 64, 1),
+        total,
+        NT,
+        precision=lax.Precision.HIGHEST,
+        preferred_element_type=F32,
+    )
+    scale = lax.rsqrt(slot_squares[:, 0:1] / D + 1e-05)
+    slot_experts = jnp.dot(mine.astype(BF16), routed_pad, preferred_element_type=F32)
+    number = iota((SLOTS, 128), 1)
+    own_logit = jnp.sum(jnp.where(number == chip, slot_logits, 0.0), axis=1, keepdims=True)
+    other_logit = jnp.sum(
+        jnp.where(number == chip, 0.0, slot_logits * slot_experts), axis=1, keepdims=True
+    )
+    weight = 1.0 / (1.0 + jnp.exp((other_logit - own_logit) * scale))
+
+    def up_step(j):
+        slot = lax.rem(j, UP_SLOTS)
+        gu_copy(j, 0).wait()
+        gu_copy(j, 1).wait()
+        rows_in = xfull[...]
+        gate_part = jnp.dot(rows_in, gu[slot, 0], preferred_element_type=F32) * scale
+        up_part = jnp.dot(rows_in, gu[slot, 1], preferred_element_type=F32) * scale
+        silu = gate_part / (1.0 + jnp.exp(-gate_part))
+        act[:, pl.ds(pl.multiple_of(j * FF_STEP, FF_STEP), FF_STEP)] = (silu * up_part).astype(BF16)
+
+    @pl.loop(0, FF_STEPS - UP_SLOTS)
+    def _(j):
+        up_step(j)
+        gu_copy(j + UP_SLOTS, 0).start()
+        gu_copy(j + UP_SLOTS, 1).start()
+
+    @pl.loop(FF_STEPS - UP_SLOTS, FF_STEPS)
+    def _(j):
+        up_step(j)
+
+    def return_copy(d, cc):
+        return remote(
+            rs.at[d, :, cc * 128 : cc * 128 + HALF_W],
+            ret.at[core, chip],
+            r_send.at[d, cc],
+            r_recv.at[core * CHIPS + chip],
+            down_chip(d) * 2 + cc,
+        )
+
+    def down_step(d):
+        dn_copy(d).wait()
+        part = jnp.dot(act[...], dn[lax.rem(d, DOWN_SLOTS)], preferred_element_type=F32)
+        rs[d] = (part * weight).astype(BF16)
+
+    @pl.loop(0, CHIPS - DOWN_SLOTS)
+    def _(d):
+        down_step(d)
+        return_copy(d, 0).start()
+        return_copy(d, 1).start()
+        dn_copy(d + DOWN_SLOTS).start()
+
+    @pl.loop(CHIPS - DOWN_SLOTS, CHIPS - 1)
+    def _(d):
+        down_step(d)
+        return_copy(d, 0).start()
+        return_copy(d, 1).start()
+
+    last = CHIPS - 1
+    down_step(last)
+
+    def to_sibling(lanes):
+        return remote(
+            rs.at[last, :, lanes],
+            ret.at[core, chip],
+            r_send.at[last, 0],
+            r_recv.at[core * CHIPS + chip],
+            sibling,
+        )
+
+    @pl.when(core == 0)
+    def _():
+        to_sibling(slice(128, 384)).start()
+        ret[core, chip] = rs[last, :, 0:256]
+
+    @pl.when(core == 1)
+    def _():
+        to_sibling(slice(0, 256)).start()
+        ret[core, chip] = rs[last, :, 128:384]
+
+    def wait_return(cc, source_chip):
+        remote(
+            rs.at[0, :, 0:HALF_W],
+            ret.at[cc, source_chip],
+            r_send.at[0, 0],
+            r_recv.at[cc * CHIPS + source_chip],
+            sibling,
+        ).wait_recv()
+
+    for k in range(1, CHIPS):
+        for cc in range(2):
+            wait_return(cc, lax.rem(chip + k, CHIPS))
+    wait_return(1 - core, chip)
+
+    table_bf = table.astype(BF16)
+    moe = jnp.zeros((ROWS, HALF_W), F32)
+    for cc in range(2):
+        moe += jnp.dot(
+            table_bf, ret[cc].reshape(EXPERTS * SLOTS, HALF_W), preferred_element_type=F32
+        )
+    moe = pltpu.roll(moe, core * (HALF_W - 64), 1)
+    out[...] = (hidden + moe[:, 0:COLS]).astype(BF16)
+
+    for copy in sent:
+        copy.wait_send()
+    for copies in sent_x:
+        for copy in copies:
+            copy.wait_send()
+
+    @pl.loop(0, last)
+    def _(d):
+        return_copy(d, 0).wait_send()
+        return_copy(d, 1).wait_send()
+
+    to_sibling(slice(0, 256)).wait_send()
+
+
+def fused(
+    residual,
+    queries,
+    kv_cache,
+    lengths,
+    out_weight,
+    norm_gain,
+    router_weight,
+    gate_weight,
+    up_weight,
+    down_weight,
+    expert_ids,
+):
+    vmem = pl.BlockSpec(memory_space=pltpu.VMEM)
+    anywhere = pl.BlockSpec(memory_space=pl.ANY)
+    dma = pltpu.SemaphoreType.DMA
+    return pl.pallas_call(
+        fused_kernel,
+        out_shape=jax.ShapeDtypeStruct((ROWS, COLS), BF16),
+        in_specs=[pl.BlockSpec(memory_space=pltpu.SMEM)] + [vmem] * 4 + [anywhere] * 6,
+        out_specs=vmem,
+        scratch_shapes=[
+            pltpu.VMEM((BLOCK_ROWS, HEADS_W), BF16),
+            pltpu.VMEM((2, BLOCK_ROWS, 128, HEAD_DIM), BF16),
+            pltpu.VMEM((KVHEADS * HEADS_W, COLS), BF16),
+            pltpu.VMEM((UP_SLOTS, 2, D, FF_STEP), BF16),
+            pltpu.VMEM((DOWN_SLOTS, FF_LOCAL, PAIR), BF16),
+            pltpu.VMEM((BLOCK_ROWS, 8, HEAD_DIM), F32),
+            pltpu.VMEM((BLOCK_ROWS, 8, 128), jnp.int32),
+            pltpu.VMEM((DEVS, BLOCK_ROWS, HEADS_W), BF16),
+            pltpu.VMEM((EXPERTS * SLOTS, 128), F32),
+            pltpu.VMEM((128, HALF_W), F32),
+            pltpu.VMEM((EXPERTS, SLOTS, HALF_W), BF16),
+            pltpu.VMEM((2, CHIPS, SLOTS, HALF_W), BF16),
+            pltpu.VMEM((8, 128), F32),
+            pltpu.VMEM((2, CHIPS, 8, 128), F32),
+            pltpu.VMEM((SLOTS, D), BF16),
+            pltpu.VMEM((SLOTS, FF_LOCAL), BF16),
+            pltpu.VMEM((CHIPS, SLOTS, PAIR), BF16),
+            pltpu.VMEM((2, CHIPS, SLOTS, HALF_W), BF16),
+            dma((3,)),
+            dma((UP_SLOTS, 2)),
+            dma((DOWN_SLOTS,)),
+            dma((DEVS,)),
+            dma((DEVS,)),
+            dma((DEVS,)),
+            dma((DEVS,)),
+            dma((DEVS,)),
+            dma((DEVS,)),
+            dma((CHIPS, 2)),
+            dma((DEVS,)),
+        ],
+        compiler_params=pltpu.CompilerParams(
+            collective_id=0, has_side_effects=True, vmem_limit_bytes=62 * 1024 * 1024
+        ),
+        cost_estimate=pl.CostEstimate(
+            flops=2 * SLOTS * 3 * D * FF_LOCAL, bytes_accessed=6 * D * FF_LOCAL, transcendentals=0
+        ),
+    )(
+        lengths,
+        expert_ids,
+        residual,
+        norm_gain.reshape(1, COLS),
+        router_weight,
+        queries,
+        kv_cache,
+        out_weight,
+        gate_weight,
+        up_weight,
+        down_weight,
+    )
+
+
 def solution(mesh):
+    body = fused if mesh.shape["dev"] == DEVS else on_device
     in_specs = (
         P("groups", "dev"),
         P(("groups", "dev"), None, None),
@@ -147,5 +626,5 @@
     )
     out_specs = P("groups", "dev")
     return jax.shard_map(
-        on_device, mesh=mesh, in_specs=in_specs, out_specs=out_specs, check_vma=False
-    )
+        body, mesh=mesh, in_specs=in_specs, out_specs=out_specs, check_vma=False
+    )

time: 162 us -> 59.8 us (0.37)
  blocking collectives: 84.8 us -> 0 us
  Pallas kernels: 0 us -> 49.5 us
  matrix products: 37.5 us -> 0 us
  waiting for transfers between devices: 22.2 us -> 0 us
  starting transfers between devices: 7.1 us -> 0 us
  other arithmetic: 2.46 us -> 0 us
  local copies, waits for them, and re-layouts: 7.57 us -> 9.89 us
    psum x2 -> x0, blocking collectives: 59.3 us -> none  [the longest x1 29.8 us: on_device(): square_total = lax.psum(squares_local, 'dev')]
    pallas_call x0 -> x1, Pallas kernels: none -> 49.5 us  [fused(): pl.pallas_call(fused_kernel, out_shape=jax.ShapeDtypeStruct((ROWS, COLS),...]
    dot_general x7 -> x0, matrix products: 35.4 us -> none  [the longest x1 19.9 us: run_expert(): jnp.dot(activation, down_weight, preferred_element_type=jnp.float32)]
    all_gather x1 -> x0, blocking collectives: 25.5 us -> none  [on_device(): gathered = lax.all_gather(heads_local, 'dev', axis=0, tiled=True)]
    all_to_all x2 -> x0, waiting for transfers between devices: 22.2 us -> none  [the longest x1 12.9 us: on_device(): lax.all_to_all(expert_out, 'dev', split_axis=1, concat_axis=1, tiled=True)]
    unnamed x5 -> x4, local copies, waits for them, and re-layouts: 0.02 us -> 8.66 us
    all_to_all x2 -> x0, starting transfers between devices: 7.1 us -> none  [the longest x1 3.57 us: on_device(): lax.all_to_all(expert_out, 'dev', split_axis=1, concat_axis=1, tiled=True)]
    gather x4 -> x0, local copies, waits for them, and re-layouts: 2.97 us -> none  [the longest x2 1.51 us: on_device(): moe = summed[first_rank, first_expert] + summed[second_rank, second_expert]]
  transfers between devices with their start and end apart: 2 -> 0, of which waited for: 2 -> 0; matrix products, arithmetic and copies ran while one was open for 1% -> 0% of each run, Pallas kernels for 0% -> 0%
where the time goes in v1:
time: 59.8 us; the launch traced here: 59.4 us
  Pallas kernels  49.5 us (83%)
  local copies, waits for them, and re-layouts  9.89 us (17%)
    pallas_call x1, Pallas kernels, fused(): pl.pallas_call(fused_kernel, out_shape=jax.ShapeDtypeStruct((ROWS, COLS),...  49.5 us
    unnamed x4, local copies, waits for them, and re-layouts  8.66 us
    reshape x1, local copies, waits for them, and re-layouts, fused(): norm_gain.reshape(1, COLS)  1.23 us

profile of v1, /device:TPU:0, one launch (start us, length us, event | category | flops | bytes accessed | tf_op | source)
XLA Modules:
  0.0 59.4 jit_solution(17333707509554365453)
XLA Ops:
  0.0 1.2 %reshape.3.gain = bf16[1,192]{1,0:T(2,128)(2,1)} reshape(bf16[192]{0:T(256)(128)(2,1)} %param.16) | data formatting | bytes 768 | tf_op jit(solution)/shard_map/reshape | solution.py:601
  1.2 1.4 %copy.12.ids = s32[64,2]{1,0:T(8,128)} copy(s32[64,2]{0,1:T(2,128)} %param.21) | data formatting | bytes 1024 | tf_op args[10]
  2.6 1.4 %copy.13.router = bf16[192,8]{1,0:T(8,128)(2,1)} copy(bf16[192,8]{0,1:T(8,128)(2,1)} %param.17) | data formatting | bytes 6144 | tf_op args[6]
  4.0 4.5 %copy.14.ow_hbm = bf16[6144,192]{1,0:T(8,128)(2,1)} copy(bf16[6144,192]{0,1:T(8,128)(2,1)} %param.15) | data formatting | bytes 4718592 | tf_op args[4]
  8.5 49.5 %shard_map.109 = bf16[64,192]{1,0:T(8,128)(2,1)} custom-call(s32[64]{0:T(128)} %lengths.1, s32[64,2]{1,0:T(8,128)} %copy.12.ids, bf16[64,192]{1,0:T(8,128)(2,1)} %residual.1, bf16[1,192]{1,0:T(2,128)(2,1)} %reshape.3.gain, bf16[192,8]{1,0:T(8,128)(2,1)} %copy.13.router, bf16[1,32,768]{2,1,0:T(8,128)(2,1)} %q_hbm.1, bf16[1,2,32,128,128]{4,3,2,1,0:T(8,128)(2,1)} %kv_hbm.1, ...), custom_call_target="tpu_custom_call" | custom-call | flops 2415919104 | bytes 75497472 | tf_op jit(solution)/shard_map/pallas_call | solution.py:555
  58.0 1.4 %copy.16 = bf16[64,192]{1,0:T(8,128)(2,1)} copy(bf16[64,192]{1,0:T(8,128)(2,1)} %shard_map.109) | data formatting | bytes 49152

commit v2 on v1

--- a/solution.py
+++ b/solution.py
@@ -147,8 +147,8 @@
 FF_LOCAL = 4096
 FF_STEP = 512
 FF_STEPS = FF_LOCAL // FF_STEP
-UP_SLOTS = 6
-DOWN_SLOTS = 5
+UP_SLOTS = 5
+DOWN_SLOTS = 8
 F32 = jnp.float32
 BF16 = jnp.bfloat16
 NT = (((1,), (1,)), ((), ()))
@@ -178,8 +178,10 @@
     dn,
     qs,
     lens,
+    ids_pad,
     heads,
     gt,
+    summed,
     wide,
     picks,
     xb,
@@ -226,6 +228,7 @@
     ow_copy = pltpu.make_async_copy(ow_hbm, ow, in_sem.at[2])
     q_copy.start()
     kv_copy.start()
+    ow_copy.start()
 
     barrier = pltpu.get_barrier_semaphore()
     for k in range(1, DEVS):
@@ -258,27 +261,27 @@
     for t in range(BLOCK_ROWS):
         lens[t] = jnp.full((8, 128), lengths[my_rows + t], jnp.int32)
 
-    lane = iota((ROWS, 128), 1)
-    routed = jnp.where((ids[:, 0:1] == lane) | (ids[:, 1:2] == lane), 1.0, 0.0)
-    tri = jnp.where(iota((ROWS, ROWS), 0) > iota((ROWS, ROWS), 1), 1.0, 0.0).astype(BF16)
-    rank = jnp.dot(tri, routed.astype(BF16), preferred_element_type=F32)
+    ids_pad[...] = jnp.full_like(ids_pad, -1)
+    ids_pad[0:2, 0:ROWS] = ids[...]
+    expert = iota((128, 128), 0)
+    routed = jnp.where((ids_pad[0:1, :] == expert) | (ids_pad[1:2, :] == expert), 1.0, 0.0)
+    before = jnp.where(expert < iota((128, 128), 1), 1.0, 0.0).astype(BF16)
+    routed_bf = routed.astype(BF16)
+    rank = jnp.dot(routed_bf, before, preferred_element_type=F32)
     code = (routed * (rank + 1.0)).astype(BF16)
-    owner = iota((128, EXPERTS * SLOTS), 0) * SLOTS
-    place = iota((128, EXPERTS * SLOTS), 1)
+    place = iota((EXPERTS * SLOTS, 128), 0)
+    owner = iota((EXPERTS * SLOTS, 128), 1) * SLOTS
     spread = jnp.where((place >= owner) & (place < owner + SLOTS), 1.0, 0.0).astype(BF16)
-    spread_code = jnp.dot(code, spread, preferred_element_type=F32)
-    slot_number = (jnp.bitwise_and(iota((ROWS, EXPERTS * SLOTS), 1), SLOTS - 1) + 1).astype(F32)
-    table = jnp.where(spread_code == slot_number, 1.0, 0.0)
-    table_pad = jnp.concatenate([table, jnp.zeros_like(table)], axis=0)
-    gt[...] = jnp.transpose(table_pad)
-    routed_pad = jnp.concatenate([routed, jnp.zeros_like(routed)], axis=0).astype(BF16)
+    spread_code = jnp.dot(spread, code, preferred_element_type=F32)
+    slot_number = (jnp.bitwise_and(place, SLOTS - 1) + 1).astype(F32)
+    gt[...] = jnp.where(spread_code == slot_number, 1.0, 0.0)
 
     q_copy.wait()
     qs[...] = jnp.zeros_like(qs)
     for j in range(GROUP_Q):
         qs[:, j, :] = q_in[:, j * HEAD_DIM : (j + 1) * HEAD_DIM].astype(F32)
     kv_copy.wait()
-    ow_copy.start()
+    ow_copy.wait()
     for j in range(UP_SLOTS):
         gu_copy(j, 0).start()
         gu_copy(j, 1).start()
@@ -311,33 +314,38 @@
         copy.start()
         sent.append(copy)
 
+    def project(block):
+        at = pl.multiple_of(lax.rem(block, KVHEADS) * HEADS_W, HEADS_W)
+        rows_at = pl.ds(pl.multiple_of(block // KVHEADS * BLOCK_ROWS, BLOCK_ROWS), BLOCK_ROWS)
+        summed[rows_at, :] += lax.dot_general(
+            heads[block], ow[:, pl.ds(at, HEADS_W)], NT, preferred_element_type=F32
+        )
+
     for k in (2, 1, 3):
         send_heads(me, dev_of(lax.rem(z + k, ZS), y, core))
     send_heads(me, dev_of(z, 1 - y, core))
     send_heads(me, sibling)
+    summed[...] = residual[...].astype(F32)
+    project(me)
     for k in (1, 3, 2):
         block = dev_of(lax.rem(z + k, ZS), y, core)
         head_copy(block, 0, sibling).wait_recv()
         send_heads(block, dev_of(z, 1 - y, core))
         send_heads(block, sibling)
+        project(block)
     for k in (0, 1, 3, 2):
         block = dev_of(lax.rem(z + k, ZS), 1 - y, core)
         head_copy(block, 0, sibling).wait_recv()
         send_heads(block, sibling)
-    for k in (0, 1, 3, 2):
-        for yy in (y, 1 - y):
+        project(block)
+    for yy in (y, 1 - y):
+        for k in (0, 1, 3, 2):
             block = dev_of(lax.rem(z + k, ZS), yy, 1 - core)
             head_copy(block, 0, sibling).wait_recv()
-
-    ow_copy.wait()
-    attended = jnp.zeros((ROWS, COLS), F32)
-    for g in range(KVHEADS):
-        both = jnp.concatenate([heads[g], heads[KVHEADS + g]], axis=0)
-        attended += jnp.dot(
-            both, ow[g * HEADS_W : (g + 1) * HEADS_W, :], preferred_element_type=F32
-        )
-    hidden = residual[...].astype(F32) + attended
-    gained = hidden * gain[...].astype(F32)
+            project(block)
+
+    hidden = summed[...]
+    gained = hidden * gain[...].astype(F32).reshape(1, COLS)
 
     wide[...] = jnp.zeros_like(wide)
     wide[0:ROWS, 0:COLS] = gained
@@ -345,12 +353,9 @@
     picked = jnp.dot(gt[...].astype(BF16), shifted.astype(BF16), preferred_element_type=F32)
     picks[...] = picked.astype(BF16).reshape(EXPERTS, SLOTS, HALF_W)
 
-    router_cols = jnp.transpose(
-        jnp.concatenate([router[...].astype(F32), jnp.zeros((COLS, 120), F32)], axis=1)
-    )[0:8]
     none = jnp.zeros_like(hidden)
     stat_out[...] = lax.dot_general(
-        router_cols,
+        router[...].astype(F32),
         jnp.concatenate([gained, none], axis=0),
         NT,
         precision=lax.Precision.HIGHEST,
@@ -422,7 +427,9 @@
         preferred_element_type=F32,
     )
     scale = lax.rsqrt(slot_squares[:, 0:1] / D + 1e-05)
-    slot_experts = jnp.dot(mine.astype(BF16), routed_pad, preferred_element_type=F32)
+    slot_experts = lax.dot_general(
+        mine.astype(BF16), routed_bf, NT, preferred_element_type=F32
+    )
     number = iota((SLOTS, 128), 1)
     own_logit = jnp.sum(jnp.where(number == chip, slot_logits, 0.0), axis=1, keepdims=True)
     other_logit = jnp.sum(
@@ -513,11 +520,11 @@
             wait_return(cc, lax.rem(chip + k, CHIPS))
     wait_return(1 - core, chip)
 
-    table_bf = table.astype(BF16)
+    table = jnp.transpose(gt[...])[0:ROWS].astype(BF16)
     moe = jnp.zeros((ROWS, HALF_W), F32)
     for cc in range(2):
         moe += jnp.dot(
-            table_bf, ret[cc].reshape(EXPERTS * SLOTS, HALF_W), preferred_element_type=F32
+            table, ret[cc].reshape(EXPERTS * SLOTS, HALF_W), preferred_element_type=F32
         )
     moe = pltpu.roll(moe, core * (HALF_W - 64), 1)
     out[...] = (hidden + moe[:, 0:COLS]).astype(BF16)
@@ -560,13 +567,15 @@
         scratch_shapes=[
             pltpu.VMEM((BLOCK_ROWS, HEADS_W), BF16),
             pltpu.VMEM((2, BLOCK_ROWS, 128, HEAD_DIM), BF16),
-            pltpu.VMEM((KVHEADS * HEADS_W, COLS), BF16),
+            pltpu.VMEM((COLS, KVHEADS * HEADS_W), BF16),
             pltpu.VMEM((UP_SLOTS, 2, D, FF_STEP), BF16),
             pltpu.VMEM((DOWN_SLOTS, FF_LOCAL, PAIR), BF16),
             pltpu.VMEM((BLOCK_ROWS, 8, HEAD_DIM), F32),
             pltpu.VMEM((BLOCK_ROWS, 8, 128), jnp.int32),
+            pltpu.VMEM((8, 128), jnp.int32),
             pltpu.VMEM((DEVS, BLOCK_ROWS, HEADS_W), BF16),
             pltpu.VMEM((EXPERTS * SLOTS, 128), F32),
+            pltpu.VMEM((ROWS, COLS), F32),
             pltpu.VMEM((128, HALF_W), F32),
             pltpu.VMEM((EXPERTS, SLOTS, HALF_W), BF16),
             pltpu.VMEM((2, CHIPS, SLOTS, HALF_W), BF16),
@@ -589,20 +598,20 @@
             dma((DEVS,)),
         ],
         compiler_params=pltpu.CompilerParams(
-            collective_id=0, has_side_effects=True, vmem_limit_bytes=62 * 1024 * 1024
+            collective_id=0, has_side_effects=True, vmem_limit_bytes=63 * 1024 * 1024
         ),
         cost_estimate=pl.CostEstimate(
             flops=2 * SLOTS * 3 * D * FF_LOCAL, bytes_accessed=6 * D * FF_LOCAL, transcendentals=0
         ),
     )(
         lengths,
-        expert_ids,
+        expert_ids.T,
         residual,
-        norm_gain.reshape(1, COLS),
-        router_weight,
+        norm_gain,
+        router_weight.T,
         queries,
         kv_cache,
-        out_weight,
+        out_weight.T,
         gate_weight,
         up_weight,
         down_weight,

time: 59.8 us -> 46.8 us (0.78)
  local copies, waits for them, and re-layouts: 9.89 us -> 1.38 us
  Pallas kernels: 49.5 us -> 45.2 us
    unnamed x4 -> x1, local copies, waits for them, and re-layouts: 8.66 us -> 1.38 us
    pallas_call x1, Pallas kernels: 49.5 us -> 45.2 us  [fused(): pl.pallas_call(fused_kernel, out_shape=jax.ShapeDtypeStruct((ROWS, COLS),...]
    reshape x1 -> x0, local copies, waits for them, and re-layouts: 1.23 us -> none  [fused(): norm_gain.reshape(1, COLS)]
where the time goes in v2:
time: 46.8 us; the launch traced here: 46.5 us
  Pallas kernels  45.2 us (97%)
  local copies, waits for them, and re-layouts  1.38 us (3%)
    pallas_call x1, Pallas kernels, fused(): pl.pallas_call(fused_kernel, out_shape=jax.ShapeDtypeStruct((ROWS, COLS),...  45.2 us
    unnamed x1, local copies, waits for them, and re-layouts  1.38 us

profile of v2, /device:TPU:0, one launch (start us, length us, event | category | flops | bytes accessed | tf_op | source)
XLA Modules:
  0.0 46.5 jit_solution(10865259840864475306)
XLA Ops:
  0.0 45.2 %shard_map.109 = bf16[64,192]{1,0:T(8,128)(2,1)} custom-call(s32[64]{0:T(128)} %lengths.1, s32[2,64]{1,0:T(2,128)} %bitcast.5, bf16[64,192]{1,0:T(8,128)(2,1)} %residual.1, bf16[192]{0:T(256)(128)(2,1)} %gain.1, bf16[8,192]{1,0:T(8,128)(2,1)} %bitcast.4, bf16[1,32,768]{2,1,0:T(8,128)(2,1)} %q_hbm.1, bf16[1,2,32,128,128]{4,3,2,1,0:T(8,128)(2,1)} %kv_hbm.1, ...), custom_call_target="tpu_custom_call" | custom-call | flops 2415919104 | bytes 75497472 | tf_op jit(solution)/shard_map/pallas_call | solution.py:562
  45.2 1.4 %copy.13 = bf16[64,192]{1,0:T(8,128)(2,1)} copy(bf16[64,192]{1,0:T(8,128)(2,1)} %shard_map.109) | data formatting | bytes 49152

commit v3 on v2

--- a/solution.py
+++ b/solution.py
@@ -147,8 +147,8 @@
 FF_LOCAL = 4096
 FF_STEP = 512
 FF_STEPS = FF_LOCAL // FF_STEP
-UP_SLOTS = 5
-DOWN_SLOTS = 8
+UP_SLOTS = 6
+DOWN_SLOTS = 6
 F32 = jnp.float32
 BF16 = jnp.bfloat16
 NT = (((1,), (1,)), ((), ()))
@@ -353,6 +353,32 @@
     picked = jnp.dot(gt[...].astype(BF16), shifted.astype(BF16), preferred_element_type=F32)
     picks[...] = picked.astype(BF16).reshape(EXPERTS, SLOTS, HALF_W)
 
+    sent_x = []
+
+    def row_copies(cc, source_chip, source, stat_source, number, device):
+        at = cc * CHIPS + source_chip
+        return (
+            remote(source, xb.at[cc, source_chip], x_send.at[number], x_recv.at[at], device),
+            remote(stat_source, stats.at[cc, source_chip], s_send.at[number], s_recv.at[at], device),
+        )
+
+    def send_rows(cc, source_chip, source, stat_source, device, first=False):
+        copies = row_copies(cc, source_chip, source, stat_source, len(sent_x), device)
+        copies[0].start()
+        if not first:
+            copies[1].start()
+        sent_x.append(copies)
+
+    def wait_rows(cc, source_chip):
+        for copy in row_copies(
+            cc, source_chip, xb.at[cc, source_chip], stats.at[cc, source_chip], 0, sibling
+        ):
+            copy.wait_recv()
+
+    for k in (4, 3, 5, 2, 6, 1, 7):
+        to = lax.rem(chip + k, CHIPS)
+        send_rows(core, chip, picks.at[to], stat_out, to * 2 + core, first=True)
+    send_rows(core, chip, picks.at[chip], stat_out, sibling, first=True)
     none = jnp.zeros_like(hidden)
     stat_out[...] = lax.dot_general(
         router[...].astype(F32),
@@ -367,32 +393,8 @@
         precision=lax.Precision.HIGHEST,
         preferred_element_type=F32,
     )
-
-    sent_x = []
-
-    def row_copies(cc, source_chip, source, stat_source, number, device):
-        at = cc * CHIPS + source_chip
-        return (
-            remote(source, xb.at[cc, source_chip], x_send.at[number], x_recv.at[at], device),
-            remote(stat_source, stats.at[cc, source_chip], s_send.at[number], s_recv.at[at], device),
-        )
-
-    def send_rows(cc, source_chip, source, stat_source, device):
-        copies = row_copies(cc, source_chip, source, stat_source, len(sent_x), device)
-        for copy in copies:
-            copy.start()
-        sent_x.append(copies)
-
-    def wait_rows(cc, source_chip):
-        for copy in row_copies(
-            cc, source_chip, xb.at[cc, source_chip], stats.at[cc, source_chip], 0, sibling
-        ):
-            copy.wait_recv()
-
-    for k in (4, 3, 5, 2, 6, 1, 7):
-        to = lax.rem(chip + k, CHIPS)
-        send_rows(core, chip, picks.at[to], stat_out, to * 2 + core)
-    send_rows(core, chip, picks.at[chip], stat_out, sibling)
+    for copies in sent_x:
+        copies[1].start()
     xb[core, chip] = picks[chip]
     stats[core, chip] = stat_out[...]
     for k in (1, 7, 2, 6, 3, 5, 4):

time: 46.8 us -> 46.9 us (level)
  no operation moved by 1% of the time
where the time goes in v3:
time: 46.9 us; the launch traced here: 46.6 us
  Pallas kernels  45.3 us (97%)
  local copies, waits for them, and re-layouts  1.38 us (3%)
    pallas_call x1, Pallas kernels, fused(): pl.pallas_call(fused_kernel, out_shape=jax.ShapeDtypeStruct((ROWS, COLS),...  45.3 us
    unnamed x1, local copies, waits for them, and re-layouts  1.38 us

profile of v3, /device:TPU:0, one launch (start us, length us, event | category | flops | bytes accessed | tf_op | source)
XLA Modules:
  0.0 46.6 jit_solution(5543978643574676752)
XLA Ops:
  0.0 45.3 %shard_map.109 = bf16[64,192]{1,0:T(8,128)(2,1)} custom-call(s32[64]{0:T(128)} %lengths.1, s32[2,64]{1,0:T(2,128)} %bitcast.5, bf16[64,192]{1,0:T(8,128)(2,1)} %residual.1, bf16[192]{0:T(256)(128)(2,1)} %gain.1, bf16[8,192]{1,0:T(8,128)(2,1)} %bitcast.4, bf16[1,32,768]{2,1,0:T(8,128)(2,1)} %q_hbm.1, bf16[1,2,32,128,128]{4,3,2,1,0:T(8,128)(2,1)} %kv_hbm.1, ...), custom_call_target="tpu_custom_call" | custom-call | flops 2415919104 | bytes 75497472 | tf_op jit(solution)/shard_map/pallas_call | solution.py:564
  45.3 1.4 %copy.13 = bf16[64,192]{1,0:T(8,128)(2,1)} copy(bf16[64,192]{1,0:T(8,128)(2,1)} %shard_map.109) | data formatting | bytes 49152
